TPU v7x, 512 devices: a whole 4x8x8 slice. The times are simulated.
512 devices in a mesh: row: 8 (over z), col: 16 (over y, core), depth: 4 (over x).
Axes of the slice: x: 4, y: 8, z: 8, core: 2. Of those that a mesh axis runs over, the one named last changes fastest.
Arguments:
- tokens: bfloat16 [4096, 8192], P(('row', 'col'), 'depth'), may hold values from -6 to 6
- gate_weight: bfloat16 [8192, 14336], P(('depth', 'row'), 'col'), may hold values from -0.0625 to 0.0625
- up_weight: bfloat16 [8192, 14336], P(('depth', 'row'), 'col'), may hold values from -0.0625 to 0.0625
- down_weight: bfloat16 [14336, 8192], P(('col', 'row'), 'depth'), may hold values from -0.125 to 0.125
- gate_keep: int32 [64, 112], replicated, may hold values from 0 to 1, as said below
- up_keep: int32 [64, 112], replicated, may hold values from 0 to 1, as said below
- down_keep: int32 [112, 64], replicated, may hold values from 0 to 1, as said below
Outputs:
- mixed: bfloat16 [4096, 8192], P(('row', 'col'), 'depth')
Inputs may be any that keep to these rules, and one draw needn't show every extreme that they name: `gate_keep`: 1 marks a kept block of the gate projection, 0 a dropped one. `up_keep`: 1 marks a kept block of the up projection, 0 a dropped one. `down_keep`: 1 marks a kept block of the down projection, 0 a dropped one.
All inputs are finite; a program needn't handle non-finite values.
Results may differ from a plain program's by a relative error of at most 0.005.
Values may be sent and summed in bfloat16 or wider, within the bound.
No kernel may reach another device: no remote copies, remote signals or barrier semaphores. Data moves between devices by JAX's collectives and lax.ppermute only.
A program may use at most 64 MiB of HBM per device.

v0:
```python
import jax
import jax.numpy as jnp
from jax import lax
from jax.sharding import PartitionSpec as P

BLOCK = 128


def keep_table(keep, row_start, col_start, row_count, col_count):
    keep_bits = keep.astype(jnp.bfloat16)
    row_ids = (row_start + jnp.arange(row_count, dtype=jnp.int32)) // BLOCK
    col_ids = (col_start + jnp.arange(col_count, dtype=jnp.int32)) // BLOCK
    pick_rows = (row_ids[:, None] == jnp.arange(keep.shape[0], dtype=jnp.int32)[None, :]).astype(
        jnp.bfloat16
    )
    pick_cols = (jnp.arange(keep.shape[1], dtype=jnp.int32)[:, None] == col_ids[None, :]).astype(
        jnp.bfloat16
    )
    inner = jnp.dot(keep_bits, pick_cols, preferred_element_type=jnp.float32).astype(jnp.bfloat16)
    return jnp.dot(pick_rows, inner, preferred_element_type=jnp.float32).astype(jnp.bfloat16)


def add_panel(token_block, piece):
    return jnp.dot(token_block, piece, preferred_element_type=jnp.float32)


def on_device(tokens, gate_weight, up_weight, down_weight, gate_keep, up_keep, down_keep):
    depth_pos = lax.axis_index("depth")
    row_pos = lax.axis_index("row")
    column_pos = lax.axis_index("col")
    row_total = lax.axis_size("row")
    feature_rows = gate_weight.shape[0]
    hidden_cols = gate_weight.shape[1]
    feature_start = (depth_pos * row_total + row_pos) * feature_rows
    hidden_start = column_pos * hidden_cols
    gate_masked = gate_weight * keep_table(
        gate_keep, feature_start, hidden_start, feature_rows, hidden_cols
    )
    up_masked = up_weight * keep_table(
        up_keep, feature_start, hidden_start, feature_rows, hidden_cols
    )
    down_rows_count = down_weight.shape[0]
    down_features = down_weight.shape[1]
    down_start = (column_pos * row_total + row_pos) * down_rows_count
    down_masked = down_weight * keep_table(
        down_keep, down_start, depth_pos * down_features, down_rows_count, down_features
    )
    token_block = lax.all_gather(tokens, "col", axis=0, tiled=True)

    def add_one(piece):
        return add_panel(token_block, piece)

    gate = add_one(lax.all_gather(gate_masked, "row", axis=0, tiled=True))
    up = add_one(lax.all_gather(up_masked, "row", axis=0, tiled=True))
    both = jnp.stack((gate, up), 0)
    total = lax.psum(both, "depth")
    hidden = (jax.nn.silu(total[0]) * total[1]).astype(jnp.bfloat16)
    down_block = lax.all_gather(down_masked, "row", axis=0, tiled=True)
    mixed = lax.psum_scatter(
        jnp.dot(hidden, down_block, preferred_element_type=jnp.float32),
        "col",
        scatter_dimension=0,
        tiled=True,
    )
    return mixed.astype(jnp.bfloat16)


def solution(mesh):
    placed = (
        P(("row", "col"), "depth"),
        P(("depth", "row"), "col"),
        P(("depth", "row"), "col"),
        P(("col", "row"), "depth"),
        P(),
        P(),
        P(),
    )
    return jax.shard_map(
        on_device, mesh=mesh, in_specs=placed, out_specs=P(("row", "col"), "depth"), check_vma=False
    )
```

profile of v0, /device:TPU:25, one launch (start us, length us, event | category | flops | bytes accessed | tf_op | source)
XLA Modules:
  0.0 393.9 jit_solution(8674119538249657588)
XLA Ops:
  6.5 0.0 copy-start
  6.5 0.0 copy-start.1
  6.5 0.0 all-gather.7.cloned.1.call-start
  6.5 0.7 all-gather.7.cloned.1.call-update
  7.3 0.0 all-gather.9.cloned.1.call-start
  7.4 2.3 fusion.4
  9.7 0.0 all-gather.9.cloned.1.call-update
  9.7 0.0 all-gather.5.cloned.1.call-start
  9.8 2.3 fusion.3
  12.1 0.0 all-gather.5.cloned.1.call-update
  12.1 0.0 all-gather.11.cloned.1.call-start
  12.2 0.0 copy-done
  12.2 0.0 copy-done.1
  12.2 1.4 fusion
  13.7 0.0 all-gather.11.cloned.1.call-update
  13.7 0.0 all-reduce.2.cloned.1.call-start
  13.7 42.2 %all-gather.7.cloned.1.call-done = bf16[512,2048]{1,0:T(8,128)(2,1)} async-done(((bf16[32,2048]{1,0:T(8,128)(2,1)}), bf16[512,2048]{1,0:T(8,128)(2,1)}) %all-gather.7.cloned.1.call-update) | async-done | bytes 2097168 | tf_op jit(solution)/shard_map/all_gather | solution.py:48
  55.9 54.2 %all-gather.9.cloned.1.call-done = bf16[2048,896]{1,0:T(8,128)(2,1)} async-done(((bf16[256,896]{1,0:T(8,128)(2,1)}), bf16[2048,896]{1,0:T(8,128)(2,1)}) %all-gather.9.cloned.1.call-update) | async-done | bytes 3670032 | tf_op jit(solution)/shard_map/all_gather | solution.py:54
  110.2 4.8 %convolution_bitcast_fusion = f32[1,512,896]{1,2,0:T(8,128)S(1)} fusion(bf16[2048,896]{1,0:T(8,128)(2,1)} %all-gather.9.cloned.1.call-done, bf16[512,2048]{1,0:T(8,128)(2,1)} %all-gather.7.cloned.1.call-done), kind=kOutput, calls=%fused_computation.8 | convolution fusion | flops 1879048192 | bytes 7602176 | tf_op jit(solution)/shard_map/dot_general | solution.py:24
  115.0 48.7 %all-gather.5.cloned.1.call-done = bf16[2048,896]{1,0:T(8,128)(2,1)} async-done(((bf16[256,896]{1,0:T(8,128)(2,1)}), bf16[2048,896]{1,0:T(8,128)(2,1)}) %all-gather.5.cloned.1.call-update) | async-done | bytes 3670032 | tf_op jit(solution)/shard_map/all_gather | solution.py:53
  163.7 4.8 %convolution_bitcast_fusion.1 = f32[1,512,896]{1,2,0:T(8,128)S(1)} fusion(bf16[2048,896]{1,0:T(8,128)(2,1)} %all-gather.5.cloned.1.call-done, bf16[512,2048]{1,0:T(8,128)(2,1)} %all-gather.7.cloned.1.call-done), kind=kOutput, calls=%fused_computation.9 | convolution fusion | flops 1879048192 | bytes 7602176 | tf_op jit(solution)/shard_map/dot_general | solution.py:24
  168.5 2.3 pad_maximum_fusion
  170.8 0.0 all-reduce.2.cloned.1.call-update
  170.9 0.0 reduce-scatter.2.cloned.1.call-start
  170.9 46.2 %all-gather.11.cloned.1.call-done = bf16[896,2048]{1,0:T(8,128)(2,1)} async-done(((bf16[112,2048]{1,0:T(8,128)(2,1)}), bf16[896,2048]{1,0:T(8,128)(2,1)}) %all-gather.11.cloned.1.call-update) | async-done | bytes 3670032 | tf_op jit(solution)/shard_map/all_gather | solution.py:58
  217.1 95.3 %all-reduce.2.cloned.1.call-done = f32[2,512,896]{1,2,0:T(8,128)} async-done(((f32[2,512,896]{1,2,0:T(8,128)}), f32[2,512,896]{1,2,0:T(8,128)}) %all-reduce.2.cloned.1.call-update) | async-done | bytes 3670032 | tf_op jit(solution)/shard_map/psum | solution.py:56
  312.4 7.7 %fusion.5 = f32[512,2048]{1,0:T(8,128)} fusion(bf16[896,2048]{1,0:T(8,128)(2,1)} %all-gather.11.cloned.1.call-done, f32[2,512,896]{1,2,0:T(8,128)} %all-reduce.2.cloned.1.call-done), kind=kOutput, calls=%fused_computation.16 | convolution fusion | flops 1881800704 | bytes 11534336 | tf_op jit(solution)/shard_map/dot_general | solution.py:60
  320.0 0.0 reduce-scatter.2.cloned.1.call-update
  320.1 65.3 %reduce-scatter.2.cloned.1.call-done = f32[32,2048]{1,0:T(8,128)} async-done(((f32[512,2048]{1,0:T(8,128)}), f32[32,2048]{1,0:T(8,128)}) %reduce-scatter.2.cloned.1.call-update) | async-done | bytes 262160 | tf_op jit(solution)/shard_map/reduce_scatter | solution.py:59
  385.4 1.6 convert_element_type.52
  (4 shorter events, 0.0 us)
Async XLA Ops:
  6.5 5.7 %copy-start = (bf16[112,2048]{1,0:T(8,128)(2,1)S(1)}, bf16[112,2048]{1,0:T(8,128)(2,1)}, u32[]{:S(2)}) copy-start(bf16[112,2048]{1,0:T(8,128)(2,1)} %param.10) | copy-start | bytes 1376260
  6.5 5.7 %copy-start.1 = (s32[112,64]{0,1:T(8,128)S(1)}, s32[112,64]{0,1:T(8,128)}, u32[]{:S(2)}) copy-start(s32[112,64]{0,1:T(8,128)} %param.13) | copy-start | bytes 86020
  6.5 49.4 %all-gather.7.cloned.1.call-start = ((), (), s32[]{:S(2)}) async-start(), calls=%async_computation.2 | async-start | bytes 2228224 | tf_op jit(solution)/shard_map/all_gather | solution.py:48
  7.3 102.9 %all-gather.9.cloned.1.call-start = ((), (), s32[]{:S(2)}) async-start(), calls=%async_computation.3 | async-start | bytes 4128768 | tf_op jit(solution)/shard_map/all_gather | solution.py:54
  9.7 154.0 %all-gather.5.cloned.1.call-start = ((), (), s32[]{:S(2)}) async-start(), calls=%async_computation.1 | async-start | bytes 4128768 | tf_op jit(solution)/shard_map/all_gather | solution.py:53
  12.1 205.0 %all-gather.11.cloned.1.call-start = ((), (), s32[]{:S(2)}) async-start(), calls=%async_computation.5 | async-start | bytes 4128768 | tf_op jit(solution)/shard_map/all_gather | solution.py:58
  13.7 298.7 %all-reduce.2.cloned.1.call-start = ((), (), s32[]{:S(2)}) async-start(), calls=%async_computation.4 | async-start | bytes 7340032 | tf_op jit(solution)/shard_map/psum | solution.py:56
  170.9 214.5 %reduce-scatter.2.cloned.1.call-start = ((), (), s32[]{:S(2)}) async-start(), calls=%async_computation.6 | async-start | bytes 4456448 | tf_op jit(solution)/shard_map/reduce_scatter | solution.py:59
Sparse Core Ops, SparseCore 0:
  9.5 46.3 all-gather.6
  58.0 52.1 all-gather.8
  112.2 51.4 all-gather.4
  165.6 51.3 all-gather.10
  219.3 93.0 all-reduce.1
  320.2 65.1 reduce-scatter.1
where the time goes:
time: 394 us
  waiting for transfers between devices  353 us (90%)
  matrix products  23.4 us (6%)
  between operations  13.5 us (3%)
  other arithmetic  4 us (1%)
    psum x1, waiting for transfers between devices, on_device(): total = lax.psum(both, 'depth')  95.3 us
    reduce_scatter x1, waiting for transfers between devices, on_device(): lax.psum_scatter(jnp.dot(hidden, down_block, preferred_element_type=jnp.f...  65.3 us
    all_gather x1, waiting for transfers between devices, on_device(): up = add_one(lax.all_gather(up_masked, 'row', axis=0, tiled=True))  54.2 us
    all_gather x1, waiting for transfers between devices, on_device(): gate = add_one(lax.all_gather(gate_masked, 'row', axis=0, tiled=True))  48.7 us
    all_gather x1, waiting for transfers between devices, on_device(): down_block = lax.all_gather(down_masked, 'row', axis=0, tiled=True)  46.2 us
    all_gather x1, waiting for transfers between devices, on_device(): token_block = lax.all_gather(tokens, 'col', axis=0, tiled=True)  42.2 us
    dot_general x2, matrix products, add_panel(): return jnp.dot(token_block, piece, preferred_element_type=jnp.float32)  9.61 us
  transfers between devices with their start and end apart: 6, of which 6 were waited for; matrix products, arithmetic and copies ran while one was open for 5% of the time, Pallas kernels for 0%

commit v1 on v0

--- a/solution.py
+++ b/solution.py
@@ -1,9 +1,25 @@
+import functools
 import jax
 import jax.numpy as jnp
 from jax import lax
 from jax.sharding import PartitionSpec as P
 
 BLOCK = 128
+
+
+def launch_cubes_for(message, named_axis):
+    n_lanes = lax.psum(1, axis_name=named_axis)
+    res = [(i0 - 1, i0) for i0 in range(1, n_lanes)] + [(n_lanes - 1, 0)]
+    u1 = message
+    nodes = [u1]
+    for _ in range(n_lanes - 1):
+        u1 = lax.ppermute(u1, axis_name=named_axis, perm=res)
+        nodes += [u1]
+    a_now = jnp.concatenate([*reversed(nodes)], 0)
+    return jnp.roll(a_now, (lax.axis_index(named_axis) + 1) * u1.shape[0], 0)
+
+
+cut_the_corner = functools.partial(launch_cubes_for, named_axis="col")
 
 
 def keep_table(keep, row_start, col_start, row_count, col_count):
@@ -45,7 +61,7 @@
     down_masked = down_weight * keep_table(
         down_keep, down_start, depth_pos * down_features, down_rows_count, down_features
     )
-    token_block = lax.all_gather(tokens, "col", axis=0, tiled=True)
+    token_block = cut_the_corner(tokens)
 
     def add_one(piece):
         return add_panel(token_block, piece)

time: 394 us -> 351 us (0.89)
  waiting for transfers between devices: 353 us -> 234 us
  starting transfers between devices: 0.21 us -> 54.3 us
  local copies, waits for them, and re-layouts: 0.01 us -> 21 us
    all_gather x1, waiting for transfers between devices: 54.2 us -> 0.02 us  [on_device(): up = add_one(lax.all_gather(up_masked, 'row', axis=0, tiled=True))]
    ppermute x0 -> x15, starting transfers between devices: none -> 54.1 us  [launch_cubes_for(): u1 = lax.ppermute(u1, axis_name=named_axis, perm=res)]
    all_gather x1, waiting for transfers between devices: 48.7 us -> 0.01 us  [on_device(): gate = add_one(lax.all_gather(gate_masked, 'row', axis=0, tiled=True))]
    all_gather x1 -> x0, waiting for transfers between devices: 42.2 us -> none  [on_device(): token_block = lax.all_gather(tokens, 'col', axis=0, tiled=True)]
    ppermute x0 -> x15, waiting for transfers between devices: none -> 27.6 us  [launch_cubes_for(): u1 = lax.ppermute(u1, axis_name=named_axis, perm=res)]
    unnamed x4 -> x33, local copies, waits for them, and re-layouts: 0.01 us -> 20.4 us
  transfers between devices with their start and end apart: 6 -> 20, of which waited for: 6 -> 17; matrix products, arithmetic and copies ran while one was open for 5% -> 11% of each run, Pallas kernels for 0% -> 0%
where the time goes in v1:
time: 351 us
  waiting for transfers between devices  234 us (67%)
  starting transfers between devices  54.3 us (15%)
  matrix products  24.7 us (7%)
  local copies, waits for them, and re-layouts  21 us (6%)
  between operations  13.2 us (4%)
  other arithmetic  3.68 us (1%)
    psum x1, waiting for transfers between devices, on_device(): total = lax.psum(both, 'depth')  95.3 us
    reduce_scatter x1, waiting for transfers between devices, on_device(): lax.psum_scatter(jnp.dot(hidden, down_block, preferred_element_type=jnp.f...  65.4 us
    ppermute x15, starting transfers between devices, launch_cubes_for(): u1 = lax.ppermute(u1, axis_name=named_axis, perm=res)  54.1 us
    all_gather x1, waiting for transfers between devices, on_device(): down_block = lax.all_gather(down_masked, 'row', axis=0, tiled=True)  45.3 us
    ppermute x15, waiting for transfers between devices, launch_cubes_for(): u1 = lax.ppermute(u1, axis_name=named_axis, perm=res)  27.6 us
    unnamed x33, local copies, waits for them, and re-layouts  20.4 us
    dot_general x2, matrix products, add_panel(): return jnp.dot(token_block, piece, preferred_element_type=jnp.float32)  9.99 us
    dot_general x1, matrix products, on_device(): jnp.dot(hidden, down_block, preferred_element_type=jnp.float32)  7.46 us
  transfers between devices with their start and end apart: 20, of which 17 were waited for; matrix products, arithmetic and copies ran while one was open for 11% of the time, Pallas kernels for 0%

profile of v1, /device:TPU:25, one launch (start us, length us, event | category | flops | bytes accessed | tf_op | source)
XLA Modules:
  0.0 350.6 jit_solution(2601957791248896709)
XLA Ops:
  6.6 2.4 fusion.13
  9.0 2.4 fusion.14
  11.5 3.1 collective-permute-start
  14.5 2.3 collective-permute-done
  16.8 3.5 %collective-permute-start.1 = (bf16[32,2048]{1,0:T(8,128)(2,1)S(1)}, bf16[32,2048]{1,0:T(8,128)(2,1)S(1)}, u32[]{:S(2)}, u32[]{:S(2)}) collective-permute-start(bf16[32,2048]{1,0:T(8,128)(2,1)S(1)} %collective-permute-done), channel_id=1, source_target_pairs={{0,4},{4,8},{8,12},{12,16},{16,20},{20,24},{24,28},{28,32},{32,36}... | collective-permute-start | bytes 393224 | tf_op jit(solution)/shard_map/ppermute | solution.py:16
  20.4 1.9 collective-permute-done.1
  22.3 3.7 %collective-permute-start.2 = (bf16[32,2048]{1,0:T(8,128)(2,1)S(1)}, bf16[32,2048]{1,0:T(8,128)(2,1)S(1)}, u32[]{:S(2)}, u32[]{:S(2)}) collective-permute-start(bf16[32,2048]{1,0:T(8,128)(2,1)S(1)} %collective-permute-done.1), channel_id=1, source_target_pairs={{0,4},{4,8},{8,12},{12,16},{16,20},{20,24},{24,28},{28,32},{32,36}... | collective-permute-start | bytes 393224 | tf_op jit(solution)/shard_map/ppermute | solution.py:16
  26.0 1.9 collective-permute-done.2
  27.9 3.7 %collective-permute-start.3 = (bf16[32,2048]{1,0:T(8,128)(2,1)S(1)}, bf16[32,2048]{1,0:T(8,128)(2,1)S(1)}, u32[]{:S(2)}, u32[]{:S(2)}) collective-permute-start(bf16[32,2048]{1,0:T(8,128)(2,1)S(1)} %collective-permute-done.2), channel_id=1, source_target_pairs={{0,4},{4,8},{8,12},{12,16},{16,20},{20,24},{24,28},{28,32},{32,36}... | collective-permute-start | bytes 393224 | tf_op jit(solution)/shard_map/ppermute | solution.py:16
  31.6 1.9 collective-permute-done.3
  33.5 3.7 %collective-permute-start.4 = (bf16[32,2048]{1,0:T(8,128)(2,1)S(1)}, bf16[32,2048]{1,0:T(8,128)(2,1)S(1)}, u32[]{:S(2)}, u32[]{:S(2)}) collective-permute-start(bf16[32,2048]{1,0:T(8,128)(2,1)S(1)} %collective-permute-done.3), channel_id=1, source_target_pairs={{0,4},{4,8},{8,12},{12,16},{16,20},{20,24},{24,28},{28,32},{32,36}... | collective-permute-start | bytes 393224 | tf_op jit(solution)/shard_map/ppermute | solution.py:16
  37.2 1.9 collective-permute-done.4
  39.1 3.7 %collective-permute-start.5 = (bf16[32,2048]{1,0:T(8,128)(2,1)S(1)}, bf16[32,2048]{1,0:T(8,128)(2,1)S(1)}, u32[]{:S(2)}, u32[]{:S(2)}) collective-permute-start(bf16[32,2048]{1,0:T(8,128)(2,1)S(1)} %collective-permute-done.4), channel_id=1, source_target_pairs={{0,4},{4,8},{8,12},{12,16},{16,20},{20,24},{24,28},{28,32},{32,36}... | collective-permute-start | bytes 393224 | tf_op jit(solution)/shard_map/ppermute | solution.py:16
  42.8 1.9 collective-permute-done.5
  44.7 3.7 %collective-permute-start.6 = (bf16[32,2048]{1,0:T(8,128)(2,1)S(1)}, bf16[32,2048]{1,0:T(8,128)(2,1)S(1)}, u32[]{:S(2)}, u32[]{:S(2)}) collective-permute-start(bf16[32,2048]{1,0:T(8,128)(2,1)S(1)} %collective-permute-done.5), channel_id=1, source_target_pairs={{0,4},{4,8},{8,12},{12,16},{16,20},{20,24},{24,28},{28,32},{32,36}... | collective-permute-start | bytes 393224 | tf_op jit(solution)/shard_map/ppermute | solution.py:16
  48.4 1.9 collective-permute-done.6
  50.3 3.7 %collective-permute-start.7 = (bf16[32,2048]{1,0:T(8,128)(2,1)S(1)}, bf16[32,2048]{1,0:T(8,128)(2,1)S(1)}, u32[]{:S(2)}, u32[]{:S(2)}) collective-permute-start(bf16[32,2048]{1,0:T(8,128)(2,1)S(1)} %collective-permute-done.6), channel_id=1, source_target_pairs={{0,4},{4,8},{8,12},{12,16},{16,20},{20,24},{24,28},{28,32},{32,36}... | collective-permute-start | bytes 393224 | tf_op jit(solution)/shard_map/ppermute | solution.py:16
  54.0 1.9 collective-permute-done.7
  55.9 3.7 %collective-permute-start.8 = (bf16[32,2048]{1,0:T(8,128)(2,1)S(1)}, bf16[32,2048]{1,0:T(8,128)(2,1)S(1)}, u32[]{:S(2)}, u32[]{:S(2)}) collective-permute-start(bf16[32,2048]{1,0:T(8,128)(2,1)S(1)} %collective-permute-done.7), channel_id=1, source_target_pairs={{0,4},{4,8},{8,12},{12,16},{16,20},{20,24},{24,28},{28,32},{32,36}... | collective-permute-start | bytes 393224 | tf_op jit(solution)/shard_map/ppermute | solution.py:16
  59.6 1.9 collective-permute-done.8
  61.5 3.7 %collective-permute-start.9 = (bf16[32,2048]{1,0:T(8,128)(2,1)S(1)}, bf16[32,2048]{1,0:T(8,128)(2,1)S(1)}, u32[]{:S(2)}, u32[]{:S(2)}) collective-permute-start(bf16[32,2048]{1,0:T(8,128)(2,1)S(1)} %collective-permute-done.8), channel_id=1, source_target_pairs={{0,4},{4,8},{8,12},{12,16},{16,20},{20,24},{24,28},{28,32},{32,36}... | collective-permute-start | bytes 393224 | tf_op jit(solution)/shard_map/ppermute | solution.py:16
  65.2 1.9 collective-permute-done.9
  67.1 3.7 %collective-permute-start.10 = (bf16[32,2048]{1,0:T(8,128)(2,1)S(1)}, bf16[32,2048]{1,0:T(8,128)(2,1)S(1)}, u32[]{:S(2)}, u32[]{:S(2)}) collective-permute-start(bf16[32,2048]{1,0:T(8,128)(2,1)S(1)} %collective-permute-done.9), channel_id=1, source_target_pairs={{0,4},{4,8},{8,12},{12,16},{16,20},{20,24},{24,28},{28,32},{32,36}... | collective-permute-start | bytes 393224 | tf_op jit(solution)/shard_map/ppermute | solution.py:16
  70.8 1.9 collective-permute-done.10
  72.7 3.7 %collective-permute-start.11 = (bf16[32,2048]{1,0:T(8,128)(2,1)S(1)}, bf16[32,2048]{1,0:T(8,128)(2,1)S(1)}, u32[]{:S(2)}, u32[]{:S(2)}) collective-permute-start(bf16[32,2048]{1,0:T(8,128)(2,1)S(1)} %collective-permute-done.10), channel_id=1, source_target_pairs={{0,4},{4,8},{8,12},{12,16},{16,20},{20,24},{24,28},{28,32},{32,36}... | collective-permute-start | bytes 393224 | tf_op jit(solution)/shard_map/ppermute | solution.py:16
  76.4 1.9 collective-permute-done.11
  78.3 3.7 %collective-permute-start.12 = (bf16[32,2048]{1,0:T(8,128)(2,1)S(1)}, bf16[32,2048]{1,0:T(8,128)(2,1)S(1)}, u32[]{:S(2)}, u32[]{:S(2)}) collective-permute-start(bf16[32,2048]{1,0:T(8,128)(2,1)S(1)} %collective-permute-done.11), channel_id=1, source_target_pairs={{0,4},{4,8},{8,12},{12,16},{16,20},{20,24},{24,28},{28,32},{32,36}... | collective-permute-start | bytes 393224 | tf_op jit(solution)/shard_map/ppermute | solution.py:16
  82.0 1.9 collective-permute-done.12
  83.9 3.7 %collective-permute-start.13 = (bf16[32,2048]{1,0:T(8,128)(2,1)S(1)}, bf16[32,2048]{1,0:T(8,128)(2,1)S(1)}, u32[]{:S(2)}, u32[]{:S(2)}) collective-permute-start(bf16[32,2048]{1,0:T(8,128)(2,1)S(1)} %collective-permute-done.12), channel_id=1, source_target_pairs={{0,4},{4,8},{8,12},{12,16},{16,20},{20,24},{24,28},{28,32},{32,36}... | collective-permute-start | bytes 393224 | tf_op jit(solution)/shard_map/ppermute | solution.py:16
  87.6 1.9 collective-permute-done.13
  89.6 3.7 %collective-permute-start.14 = (bf16[32,2048]{1,0:T(8,128)(2,1)S(1)}, bf16[32,2048]{1,0:T(8,128)(2,1)S(1)}, u32[]{:S(2)}, u32[]{:S(2)}) collective-permute-start(bf16[32,2048]{1,0:T(8,128)(2,1)S(1)} %collective-permute-done.13), channel_id=1, source_target_pairs={{0,4},{4,8},{8,12},{12,16},{16,20},{20,24},{24,28},{28,32},{32,36}... | collective-permute-start | bytes 393224 | tf_op jit(solution)/shard_map/ppermute | solution.py:16
  93.2 2.5 fusion
  96.5 0.7 constant_dynamic-update-slice_fusion.30
  97.1 0.7 constant_dynamic-update-slice_fusion.29
  97.8 0.7 constant_dynamic-update-slice_fusion.28
  98.4 0.7 constant_dynamic-update-slice_fusion.27
  99.1 0.7 constant_dynamic-update-slice_fusion.26
  99.7 0.7 constant_dynamic-update-slice_fusion.25
  100.4 0.7 constant_dynamic-update-slice_fusion.24
  101.1 0.7 constant_dynamic-update-slice_fusion.23
  101.7 0.7 constant_dynamic-update-slice_fusion.22
  102.4 0.7 constant_dynamic-update-slice_fusion.21
  103.1 0.7 constant_dynamic-update-slice_fusion.20
  104.4 0.7 constant_dynamic-update-slice_fusion.18
  105.0 0.7 constant_dynamic-update-slice_fusion.17
  105.7 0.7 constant_dynamic-update-slice_fusion.16
  106.4 0.7 constant_dynamic-update-slice_fusion.15
  107.7 0.7 constant_dynamic-update-slice_fusion.13
  108.3 0.7 constant_dynamic-update-slice_fusion.12
  109.0 0.7 constant_dynamic-update-slice_fusion.11
  109.7 0.7 constant_dynamic-update-slice_fusion.10
  110.3 0.7 constant_dynamic-update-slice_fusion.9
  111.0 0.7 constant_dynamic-update-slice_fusion.8
  112.9 0.7 constant_dynamic-update-slice_fusion.5
  113.6 0.7 constant_dynamic-update-slice_fusion.4
  116.2 0.7 constant_dynamic-update-slice_fusion
  116.9 5.0 %fusion.7 = f32[1,512,896]{2,1,0:T(8,128)S(1)} fusion(bf16[2048,896]{1,0:T(8,128)(2,1)} %all-gather.4.cloned.1.call-done, bf16[1024,2048]{1,0:T(8,128)(2,1)} %constant_dynamic-update-slice_fusion, s32[]{:T(128)S(6)} %select_n.52), kind=kOutput, calls=%fused_computation.12 | convolution fusion | flops 1879048192 | bytes 7602180 | tf_op jit(solution)/shard_map/dot_general | solution.py:40
  121.9 5.0 %fusion.10 = f32[1,512,896]{2,1,0:T(8,128)S(1)} fusion(bf16[2048,896]{1,0:T(8,128)(2,1)} %all-gather.6.cloned.1.call-done, bf16[1024,2048]{1,0:T(8,128)(2,1)} %constant_dynamic-update-slice_fusion, s32[]{:T(128)S(6)} %select_n.52), kind=kOutput, calls=%fused_computation.13 | convolution fusion | flops 1879048192 | bytes 7602180 | tf_op jit(solution)/shard_map/dot_general | solution.py:40
  126.9 2.0 pad_maximum_fusion
  129.0 45.3 %all-gather.8.cloned.1.call-done = bf16[896,2048]{1,0:T(8,128)(2,1)} async-done(((bf16[112,2048]{1,0:T(8,128)(2,1)}), bf16[896,2048]{1,0:T(8,128)(2,1)}) %all-gather.8.cloned.1.call-update) | async-done | bytes 3670032 | tf_op jit(solution)/shard_map/all_gather | solution.py:74
  174.2 95.3 %all-reduce.2.cloned.1.call-done = f32[2,512,896]{2,1,0:T(8,128)} async-done(((f32[2,512,896]{2,1,0:T(8,128)}), f32[2,512,896]{2,1,0:T(8,128)}) %all-reduce.2.cloned.1.call-update) | async-done | bytes 3670032 | tf_op jit(solution)/shard_map/psum | solution.py:72
  269.6 7.5 %fusion.15 = f32[512,2048]{1,0:T(8,128)} fusion(bf16[896,2048]{1,0:T(8,128)(2,1)} %all-gather.8.cloned.1.call-done, f32[2,512,896]{2,1,0:T(8,128)} %all-reduce.2.cloned.1.call-done), kind=kOutput, calls=%fused_computation.20 | convolution fusion | flops 1881800704 | bytes 11534336 | tf_op jit(solution)/shard_map/dot_general | solution.py:76
  277.0 65.4 %reduce-scatter.2.cloned.1.call-done = f32[32,2048]{1,0:T(8,128)} async-done(((f32[512,2048]{1,0:T(8,128)}), f32[32,2048]{1,0:T(8,128)}) %reduce-scatter.2.cloned.1.call-update) | async-done | bytes 262160 | tf_op jit(solution)/shard_map/reduce_scatter | solution.py:75
  342.4 1.6 convert_element_type.52
  (27 shorter events, 5.5 us)
Async XLA Ops:
  6.5 99.2 %copy-start = (bf16[32,2048]{1,0:T(8,128)(2,1)S(1)}, bf16[32,2048]{1,0:T(8,128)(2,1)}, u32[]{:S(2)}) copy-start(bf16[32,2048]{1,0:T(8,128)(2,1)} %param.7) | copy-start | bytes 393220
  6.5 110.3 %all-gather.4.cloned.1.call-start = ((), (), s32[]{:S(2)}) async-start(), calls=%async_computation.1 | async-start | bytes 4128768 | tf_op jit(solution)/shard_map/all_gather | solution.py:69
  9.0 112.9 %all-gather.6.cloned.1.call-start = ((), (), s32[]{:S(2)}) async-start(), calls=%async_computation.2 | async-start | bytes 4128768 | tf_op jit(solution)/shard_map/all_gather | solution.py:70
  11.4 162.8 %all-gather.8.cloned.1.call-start = ((), (), s32[]{:S(2)}) async-start(), calls=%async_computation.4 | async-start | bytes 4128768 | tf_op jit(solution)/shard_map/all_gather | solution.py:74
  11.5 5.3 %collective-permute-start = (bf16[32,2048]{1,0:T(8,128)(2,1)}, bf16[32,2048]{1,0:T(8,128)(2,1)S(1)}, u32[]{:S(2)}, u32[]{:S(2)}) collective-permute-start(bf16[32,2048]{1,0:T(8,128)(2,1)} %param.7), channel_id=1, source_target_pairs={{0,4},{4,8},{8,12},{12,16},{16,20},{20,24},{24,28},{28,32},{32,36}... | collective-permute-start | bytes 393224 | tf_op jit(solution)/shard_map/ppermute | solution.py:16
  16.8 5.5 %collective-permute-start.1 = (bf16[32,2048]{1,0:T(8,128)(2,1)S(1)}, bf16[32,2048]{1,0:T(8,128)(2,1)S(1)}, u32[]{:S(2)}, u32[]{:S(2)}) collective-permute-start(bf16[32,2048]{1,0:T(8,128)(2,1)S(1)} %collective-permute-done), channel_id=1, source_target_pairs={{0,4},{4,8},{8,12},{12,16},{16,20},{20,24},{24,28},{28,32},{32,36}... | collective-permute-start | bytes 393224 | tf_op jit(solution)/shard_map/ppermute | solution.py:16
  22.3 5.6 %collective-permute-start.2 = (bf16[32,2048]{1,0:T(8,128)(2,1)S(1)}, bf16[32,2048]{1,0:T(8,128)(2,1)S(1)}, u32[]{:S(2)}, u32[]{:S(2)}) collective-permute-start(bf16[32,2048]{1,0:T(8,128)(2,1)S(1)} %collective-permute-done.1), channel_id=1, source_target_pairs={{0,4},{4,8},{8,12},{12,16},{16,20},{20,24},{24,28},{28,32},{32,36}... | collective-permute-start | bytes 393224 | tf_op jit(solution)/shard_map/ppermute | solution.py:16
  27.9 5.6 %collective-permute-start.3 = (bf16[32,2048]{1,0:T(8,128)(2,1)S(1)}, bf16[32,2048]{1,0:T(8,128)(2,1)S(1)}, u32[]{:S(2)}, u32[]{:S(2)}) collective-permute-start(bf16[32,2048]{1,0:T(8,128)(2,1)S(1)} %collective-permute-done.2), channel_id=1, source_target_pairs={{0,4},{4,8},{8,12},{12,16},{16,20},{20,24},{24,28},{28,32},{32,36}... | collective-permute-start | bytes 393224 | tf_op jit(solution)/shard_map/ppermute | solution.py:16
  33.5 5.6 %collective-permute-start.4 = (bf16[32,2048]{1,0:T(8,128)(2,1)S(1)}, bf16[32,2048]{1,0:T(8,128)(2,1)S(1)}, u32[]{:S(2)}, u32[]{:S(2)}) collective-permute-start(bf16[32,2048]{1,0:T(8,128)(2,1)S(1)} %collective-permute-done.3), channel_id=1, source_target_pairs={{0,4},{4,8},{8,12},{12,16},{16,20},{20,24},{24,28},{28,32},{32,36}... | collective-permute-start | bytes 393224 | tf_op jit(solution)/shard_map/ppermute | solution.py:16
  39.1 5.6 %collective-permute-start.5 = (bf16[32,2048]{1,0:T(8,128)(2,1)S(1)}, bf16[32,2048]{1,0:T(8,128)(2,1)S(1)}, u32[]{:S(2)}, u32[]{:S(2)}) collective-permute-start(bf16[32,2048]{1,0:T(8,128)(2,1)S(1)} %collective-permute-done.4), channel_id=1, source_target_pairs={{0,4},{4,8},{8,12},{12,16},{16,20},{20,24},{24,28},{28,32},{32,36}... | collective-permute-start | bytes 393224 | tf_op jit(solution)/shard_map/ppermute | solution.py:16
  44.7 5.6 %collective-permute-start.6 = (bf16[32,2048]{1,0:T(8,128)(2,1)S(1)}, bf16[32,2048]{1,0:T(8,128)(2,1)S(1)}, u32[]{:S(2)}, u32[]{:S(2)}) collective-permute-start(bf16[32,2048]{1,0:T(8,128)(2,1)S(1)} %collective-permute-done.5), channel_id=1, source_target_pairs={{0,4},{4,8},{8,12},{12,16},{16,20},{20,24},{24,28},{28,32},{32,36}... | collective-permute-start | bytes 393224 | tf_op jit(solution)/shard_map/ppermute | solution.py:16
  50.3 5.6 %collective-permute-start.7 = (bf16[32,2048]{1,0:T(8,128)(2,1)S(1)}, bf16[32,2048]{1,0:T(8,128)(2,1)S(1)}, u32[]{:S(2)}, u32[]{:S(2)}) collective-permute-start(bf16[32,2048]{1,0:T(8,128)(2,1)S(1)} %collective-permute-done.6), channel_id=1, source_target_pairs={{0,4},{4,8},{8,12},{12,16},{16,20},{20,24},{24,28},{28,32},{32,36}... | collective-permute-start | bytes 393224 | tf_op jit(solution)/shard_map/ppermute | solution.py:16
  55.9 5.6 %collective-permute-start.8 = (bf16[32,2048]{1,0:T(8,128)(2,1)S(1)}, bf16[32,2048]{1,0:T(8,128)(2,1)S(1)}, u32[]{:S(2)}, u32[]{:S(2)}) collective-permute-start(bf16[32,2048]{1,0:T(8,128)(2,1)S(1)} %collective-permute-done.7), channel_id=1, source_target_pairs={{0,4},{4,8},{8,12},{12,16},{16,20},{20,24},{24,28},{28,32},{32,36}... | collective-permute-start | bytes 393224 | tf_op jit(solution)/shard_map/ppermute | solution.py:16
  61.5 5.6 %collective-permute-start.9 = (bf16[32,2048]{1,0:T(8,128)(2,1)S(1)}, bf16[32,2048]{1,0:T(8,128)(2,1)S(1)}, u32[]{:S(2)}, u32[]{:S(2)}) collective-permute-start(bf16[32,2048]{1,0:T(8,128)(2,1)S(1)} %collective-permute-done.8), channel_id=1, source_target_pairs={{0,4},{4,8},{8,12},{12,16},{16,20},{20,24},{24,28},{28,32},{32,36}... | collective-permute-start | bytes 393224 | tf_op jit(solution)/shard_map/ppermute | solution.py:16
  67.1 5.6 %collective-permute-start.10 = (bf16[32,2048]{1,0:T(8,128)(2,1)S(1)}, bf16[32,2048]{1,0:T(8,128)(2,1)S(1)}, u32[]{:S(2)}, u32[]{:S(2)}) collective-permute-start(bf16[32,2048]{1,0:T(8,128)(2,1)S(1)} %collective-permute-done.9), channel_id=1, source_target_pairs={{0,4},{4,8},{8,12},{12,16},{16,20},{20,24},{24,28},{28,32},{32,36}... | collective-permute-start | bytes 393224 | tf_op jit(solution)/shard_map/ppermute | solution.py:16
  72.7 5.6 %collective-permute-start.11 = (bf16[32,2048]{1,0:T(8,128)(2,1)S(1)}, bf16[32,2048]{1,0:T(8,128)(2,1)S(1)}, u32[]{:S(2)}, u32[]{:S(2)}) collective-permute-start(bf16[32,2048]{1,0:T(8,128)(2,1)S(1)} %collective-permute-done.10), channel_id=1, source_target_pairs={{0,4},{4,8},{8,12},{12,16},{16,20},{20,24},{24,28},{28,32},{32,36}... | collective-permute-start | bytes 393224 | tf_op jit(solution)/shard_map/ppermute | solution.py:16
  78.3 5.6 %collective-permute-start.12 = (bf16[32,2048]{1,0:T(8,128)(2,1)S(1)}, bf16[32,2048]{1,0:T(8,128)(2,1)S(1)}, u32[]{:S(2)}, u32[]{:S(2)}) collective-permute-start(bf16[32,2048]{1,0:T(8,128)(2,1)S(1)} %collective-permute-done.11), channel_id=1, source_target_pairs={{0,4},{4,8},{8,12},{12,16},{16,20},{20,24},{24,28},{28,32},{32,36}... | collective-permute-start | bytes 393224 | tf_op jit(solution)/shard_map/ppermute | solution.py:16
  83.9 5.6 %collective-permute-start.13 = (bf16[32,2048]{1,0:T(8,128)(2,1)S(1)}, bf16[32,2048]{1,0:T(8,128)(2,1)S(1)}, u32[]{:S(2)}, u32[]{:S(2)}) collective-permute-start(bf16[32,2048]{1,0:T(8,128)(2,1)S(1)} %collective-permute-done.12), channel_id=1, source_target_pairs={{0,4},{4,8},{8,12},{12,16},{16,20},{20,24},{24,28},{28,32},{32,36}... | collective-permute-start | bytes 393224 | tf_op jit(solution)/shard_map/ppermute | solution.py:16
  89.6 6.2 %collective-permute-start.14 = (bf16[32,2048]{1,0:T(8,128)(2,1)S(1)}, bf16[32,2048]{1,0:T(8,128)(2,1)S(1)}, u32[]{:S(2)}, u32[]{:S(2)}) collective-permute-start(bf16[32,2048]{1,0:T(8,128)(2,1)S(1)} %collective-permute-done.13), channel_id=1, source_target_pairs={{0,4},{4,8},{8,12},{12,16},{16,20},{20,24},{24,28},{28,32},{32,36}... | collective-permute-start | bytes 393224 | tf_op jit(solution)/shard_map/ppermute | solution.py:16
  95.7 173.8 %all-reduce.2.cloned.1.call-start = ((), (), s32[]{:S(2)}) async-start(), calls=%async_computation.3 | async-start | bytes 7340032 | tf_op jit(solution)/shard_map/psum | solution.py:72
  128.9 213.5 %reduce-scatter.2.cloned.1.call-start = ((), (), s32[]{:S(2)}) async-start(), calls=%async_computation.5 | async-start | bytes 4456448 | tf_op jit(solution)/shard_map/reduce_scatter | solution.py:75
Sparse Core Ops, SparseCore 0:
  9.4 57.7 all-gather.3
  69.3 51.3 all-gather.5
  122.8 51.3 all-gather.7
  176.5 93.0 all-reduce.1
  277.2 65.1 reduce-scatter.1
